TPU v7x, 32 devices: a whole 2x2x4 slice. The times are simulated.
32 devices in a mesh: grp: 2 (over y), ctx: 4 (over z), head: 4 (over x, core).
Axes of the slice: x: 2, y: 2, z: 4, core: 2. Of those that a mesh axis runs over, the one named last changes fastest.
Arguments:
- queries: bfloat16 [16384, 2048], P(('grp', 'ctx', 'head')), parts along dimension 0, may hold values from -6 to 6
- keys: bfloat16 [16384, 2048], P(('grp', 'ctx', 'head')), parts along dimension 0, may hold values from -6 to 6
- values: bfloat16 [16384, 2048], P(('grp', 'ctx', 'head')), parts along dimension 0, may hold values from -6 to 6
- out_grad: bfloat16 [16384, 2048], P(('grp', 'ctx', 'head')), parts along dimension 0, may hold values from -6 to 6
- level_table: float32 [8, 21, 16], P(None, None, 'head'), may hold values from 0.25 to 2
- selector: int32 [256], P(('grp', 'ctx')), parts along dimension 0, may hold values from 0 to 7
Outputs:
- attn_out: bfloat16 [16384, 2048], P(('grp', 'ctx', 'head')), parts along dimension 0
- query_grad: bfloat16 [16384, 2048], P(('grp', 'ctx', 'head')), parts along dimension 0
- key_grad: bfloat16 [16384, 2048], P(('grp', 'ctx', 'head')), parts along dimension 0
- value_grad: bfloat16 [16384, 2048], P(('grp', 'ctx', 'head')), parts along dimension 0
There are 2 independent parts, one for each index of `grp`. A program takes and returns all parts, laid end to end along the dimension named above; an argument that names none is the same for every part. Nothing has to cross between parts.
Inputs may be any that keep to these rules, and one draw needn't show every extreme that they name: `selector`: each stretch's row of the weight table.
All inputs are finite; a program needn't handle non-finite values.
Results may differ from a plain program's by a relative error of at most 0.0051.
Values may be sent and summed in bfloat16 or wider, within the bound.
A program may use at most 256 MiB of HBM per device.

v0:
```python
import math
import jax
import jax.numpy as jnp
from jax import lax
from jax.sharding import PartitionSpec as P

HIGHEST = lax.Precision.HIGHEST


def level_of(xor_value, limit):
    count = jnp.zeros(xor_value.shape, jnp.int32)
    power = 1
    while power < limit:
        count = count + (xor_value >= power).astype(jnp.int32)
        power = power * 2
    return count


def level_weights(level_table, selector, head_width):
    table_rows = jnp.arange(level_table.shape[0], dtype=jnp.int32)
    onehot = (selector[:, None] == table_rows[None, :]).astype(jnp.float32)
    per_stretch = jnp.einsum("cs,slh->clh", onehot, level_table, precision=HIGHEST)
    level_ids = jnp.arange(level_table.shape[1], dtype=jnp.int32).astype(jnp.float32)
    scaling = jnp.exp2(-0.5 * jnp.maximum(level_ids - 1.0, 0.0)) / math.sqrt(head_width)
    return per_stretch * scaling[None, :, None]


def shards(queries, keys, values, out_grad, level_table, selector):
    query_flat, key_flat, value_flat, grad_flat = (
        lax.all_to_all(queries, "head", split_axis=1, concat_axis=0, tiled=True),
        lax.all_to_all(keys, "head", split_axis=1, concat_axis=0, tiled=True),
        lax.all_to_all(values, "head", split_axis=1, concat_axis=0, tiled=True),
        lax.all_to_all(out_grad, "head", split_axis=1, concat_axis=0, tiled=True),
    )
    heads_here = level_table.shape[2]
    tok_count = query_flat.shape[0]
    head_width = query_flat.shape[1] // heads_here
    head_shape = (tok_count, heads_here, head_width)
    query_heads = query_flat.reshape(head_shape)
    key_heads = key_flat.reshape(head_shape)
    value_heads = value_flat.reshape(head_shape)
    grad_heads = grad_flat.reshape(head_shape)
    stretch_count = selector.shape[0]
    stretch_len = tok_count // stretch_count
    per_stretch = level_weights(level_table, selector, head_width)
    lower = tok_count.bit_length() - 1
    token_weights = jnp.repeat(
        jnp.transpose(per_stretch[:, : lower + 1, :], (2, 0, 1)), stretch_len, axis=1
    )
    block_rows = min(512, tok_count)
    positions = jnp.arange(tok_count, dtype=jnp.int32)
    out_parts = []
    query_parts = []
    key_total = jnp.zeros(head_shape, jnp.float32)
    value_total = jnp.zeros(head_shape, jnp.float32)
    for block_index in range(tok_count // block_rows):
        start = block_index * block_rows
        finish = start + block_rows
        query_block = query_heads[start:finish]
        grad_block = grad_heads[start:finish]
        key_part = key_heads[:finish]
        value_part = value_heads[:finish]
        row_pos = positions[start:finish]
        col_pos = positions[:finish]
        level_index = level_of(jnp.bitwise_xor(row_pos[:, None], col_pos[None, :]), tok_count)
        row_weights = token_weights[:, start:finish, :]
        weight = jnp.zeros((heads_here, block_rows, finish), jnp.float32)
        for level_id in range(lower + 1):
            weight = jnp.where(
                (level_index == level_id)[None], row_weights[:, :, level_id][:, :, None], weight
            )
        weight = jnp.where((col_pos[None, :] <= row_pos[:, None])[None], weight, 0.0)
        scores = jnp.einsum(
            "thd,shd->hts", query_block, key_part, preferred_element_type=jnp.float32
        )
        attn_weights = (scores * weight).astype(jnp.bfloat16)
        out_parts.append(
            jnp.einsum("hts,shd->thd", attn_weights, value_part, preferred_element_type=jnp.float32)
        )
        grad_scores = jnp.einsum(
            "thd,shd->hts", grad_block, value_part, preferred_element_type=jnp.float32
        )
        score_grads = (grad_scores * weight).astype(jnp.bfloat16)
        query_parts.append(
            jnp.einsum("hts,shd->thd", score_grads, key_part, preferred_element_type=jnp.float32)
        )
        padding = ((0, tok_count - finish), (0, 0), (0, 0))
        key_total = key_total + jnp.pad(
            jnp.einsum(
                "hts,thd->shd", score_grads, query_block, preferred_element_type=jnp.float32
            ),
            padding,
        )
        value_total = value_total + jnp.pad(
            jnp.einsum(
                "hts,thd->shd", attn_weights, grad_block, preferred_element_type=jnp.float32
            ),
            padding,
        )
    out_local = jnp.concatenate(out_parts, axis=0)
    query_local = jnp.concatenate(query_parts, axis=0)
    stretch_shape = (stretch_count, stretch_len, heads_here, head_width)
    stretch_query = query_heads.reshape(stretch_shape)
    stretch_grad = grad_heads.reshape(stretch_shape)
    block_state = jnp.einsum(
        "shd,she->hde", key_heads, value_heads, preferred_element_type=jnp.float32
    )
    stretch_outer = jnp.einsum(
        "cthd,cthe->chde", stretch_query, stretch_grad, preferred_element_type=jnp.float32
    )
    bits = lax.axis_size("ctx").bit_length() - 1
    cross_weights = per_stretch[:, lower + 1 : lower + 1 + bits, :]
    adjoint_terms = jnp.einsum("cjh,chde->jhde", cross_weights, stretch_outer, precision=HIGHEST)
    position = lax.axis_index("ctx")
    packet = jnp.concatenate([block_state[None], adjoint_terms], axis=0)
    gathered = lax.all_gather(packet, "ctx", axis=0, tiled=True)
    ranks = lax.axis_size("ctx")
    gathered = gathered.reshape(ranks, bits + 1, heads_here, head_width, head_width)
    bit_ids = jnp.arange(bits, dtype=jnp.int32)
    rank_ids = jnp.arange(ranks, dtype=jnp.int32)
    upper_bits = position >> bit_ids & 1
    low_start = position >> bit_ids + 1 << bit_ids + 1
    span_size = jnp.left_shift(jnp.ones_like(bit_ids), bit_ids)
    inside_low = (rank_ids[None, :] >= low_start[:, None]) & (
        rank_ids[None, :] < (low_start + span_size)[:, None]
    )
    inside_high = (rank_ids[None, :] >= (low_start + span_size)[:, None]) & (
        rank_ids[None, :] < (low_start + 2 * span_size)[:, None]
    )
    forward_mask = (inside_low & (upper_bits[:, None] == 1)).astype(jnp.float32)
    backward_mask = (inside_high & (upper_bits[:, None] == 0)).astype(jnp.float32)
    level_stack = jnp.einsum("jn,nhde->jhde", forward_mask, gathered[:, 0], precision=HIGHEST)
    returned = jnp.einsum("jn,njhde->hde", backward_mask, gathered[:, 1:], precision=HIGHEST)
    mixed = jnp.einsum("cjh,jhde->chde", cross_weights, level_stack, precision=HIGHEST).astype(
        jnp.bfloat16
    )
    returned_low = returned.astype(jnp.bfloat16)
    out_cross = jnp.einsum(
        "cthd,chde->cthe", stretch_query, mixed, preferred_element_type=jnp.float32
    ).reshape(head_shape)
    query_cross = jnp.einsum(
        "cthe,chde->cthd", stretch_grad, mixed, preferred_element_type=jnp.float32
    ).reshape(head_shape)
    key_cross = jnp.einsum(
        "she,hde->shd", value_heads, returned_low, preferred_element_type=jnp.float32
    )
    value_cross = jnp.einsum(
        "shd,hde->she", key_heads, returned_low, preferred_element_type=jnp.float32
    )
    flat_shape = (tok_count, heads_here * head_width)
    attn_rows = (out_local + out_cross).astype(jnp.bfloat16).reshape(flat_shape)
    query_rows = (query_local + query_cross).astype(jnp.bfloat16).reshape(flat_shape)
    key_rows = (key_total + key_cross).astype(jnp.bfloat16).reshape(flat_shape)
    value_rows = (value_total + value_cross).astype(jnp.bfloat16).reshape(flat_shape)
    return (
        lax.all_to_all(attn_rows, "head", split_axis=0, concat_axis=1, tiled=True),
        lax.all_to_all(query_rows, "head", split_axis=0, concat_axis=1, tiled=True),
        lax.all_to_all(key_rows, "head", split_axis=0, concat_axis=1, tiled=True),
        lax.all_to_all(value_rows, "head", split_axis=0, concat_axis=1, tiled=True),
    )


def solution(mesh):
    in_specs = (
        P(("grp", "ctx", "head"), None),
        P(("grp", "ctx", "head"), None),
        P(("grp", "ctx", "head"), None),
        P(("grp", "ctx", "head"), None),
        P(None, None, "head"),
        P(("grp", "ctx")),
    )
    out_specs = (
        P(("grp", "ctx", "head"), None),
        P(("grp", "ctx", "head"), None),
        P(("grp", "ctx", "head"), None),
        P(("grp", "ctx", "head"), None),
    )
    return jax.shard_map(shards, mesh=mesh, in_specs=in_specs, out_specs=out_specs, check_vma=False)
```

profile of v0, /device:TPU:0, one launch (start us, length us, event | category | flops | bytes accessed | tf_op | source)
XLA Modules:
  0.0 549.9 jit_solution(6099098687646648184)
XLA Ops:
  11.1 4.2 all-to-all-start
  19.3 10.5 %broadcast_compare_fusion.24 = (pred[512,1536]{1,0:T(8,128)(4,1)}, pred[512,1536]{1,0:T(8,128)(4,1)}, pred[512,1536]{1,0:T(8,128)(4,1)}, pred[512,1536]{1,0:T(8,...) fusion(s32[1536]{0:T(1024)S(1)} %iota_add_fusion, ...), kind=kLoop, calls=%fused_computation.118 | loop fusion | flops 36175872 | bytes 10231808 | tf_op jit(solution)/shard_map/le | solution.py:72
  29.8 11.2 %all-to-all-done = bf16[512,4,512]{0,2,1:T(8,128)(2,1)S(1)} async-done(((bf16[512,4,512]{0,2,1:T(8,128)(2,1)}), bf16[512,4,512]{0,2,1:T(8,128)(2,1)S(1)}, u32[]{:S(2)}, u32[]{:S(2)}) %all-to-all-start) | async-done | bytes 2097184 | tf_op jit(solution)/shard_map/all_to_all | solution.py:30
  46.0 15.1 %iota_compare_fusion = (pred[512,2048]{1,0:T(8,128)(4,1)}, pred[512,2048]{1,0:T(8,128)(4,1)}, pred[512,2048]{1,0:T(8,128)(4,1)}, pred[512,2048]{1,0:T(8,128)(4,1...) fusion(s32[512]{0:T(512)S(1)} %iota_add_fusion.2), kind=kLoop, calls=%fused_computation.69 | loop fusion | flops 48234496 | bytes 13633536 | tf_op jit(solution)/shard_map/le | solution.py:72
  71.6 4.5 all-to-all-start.2
  78.1 4.2 broadcast_compare_fusion.50
  82.3 19.5 %all-to-all-done.2 = bf16[512,4,512]{2,0,1:T(8,128)(2,1)} async-done(((bf16[512,4,512]{2,0,1:T(8,128)(2,1)}), bf16[512,4,512]{2,0,1:T(8,128)(2,1)}, u32[]{:S(2)}, u32[]{:S(2)}) %all-to-all-start.2) | async-done | bytes 2097184 | tf_op jit(solution)/shard_map/all_to_all | solution.py:32
  101.8 4.5 all-to-all-start.3
  106.8 8.4 %broadcast_compare_fusion.37 = (pred[512,1024]{1,0:T(8,128)(4,1)}, pred[512,1024]{1,0:T(8,128)(4,1)}, pred[512,1024]{1,0:T(8,128)(4,1)}, pred[512,1024]{1,0:T(8,...) fusion(s32[1024]{0:T(1024)S(1)} %iota_add_fusion.1, ...), kind=kLoop, calls=%fused_computation.141 | loop fusion | flops 24117248 | bytes 6821888 | tf_op jit(solution)/shard_map/le | solution.py:72
  134.3 4.3 copy.218
  149.9 4.8 copy.324
  154.8 5.4 reshape.1384
  172.4 4.3 reshape_reshape.7
  177.0 8.1 %multiply_convert_fusion.6 = bf16[4,512,512]{2,1,0:T(8,128)(2,1)S(1)} fusion(bf16[512,4,128]{0,2,1:T(8,128)(2,1)} %bitcast.305, bf16[512,4,128]{0,2,1:T(8,128)(2,1)} %bitcast.298, f32[4,512]{1,0:T(4,128)S(1)} %copy-done.116, f32[4,512]{1,0:T(4,128)} %get-tuple-element.60, f32[4,512]{1,0:T(4,128)} %get-tuple-element.61, f32[4,512]{1,0:T(4,128)} %get-tuple-element.62, ...), kind=kOutput, calls=%fused_computation.53 | convolution fusion | flops 284164096 | bytes 6651904 | tf_op jit(solution)/shard_map/thd,shd->hts/dot_general | solution.py:80
  185.5 6.6 %multiply_convert_fusion.7 = bf16[4,512,512]{2,1,0:T(8,128)(2,1)S(1)} fusion(bf16[512,4,128]{0,2,1:T(8,128)(2,1)S(1)} %bitcast.310, bf16[512,4,128]{0,2,1:T(8,128)(2,1)S(1)} %bitcast.296, f32[4,512]{1,0:T(4,128)S(1)} %copy-done.116, f32[4,512]{1,0:T(4,128)S(1)} %copy-done.117, f32[4,512]{1,0:T(4,128)S(1)} %copy-done.118, f32[4,512]{1,0:T(4,128)S(1)} %copy-done.119, ...), kind=kOutput, calls=%fused_computation.70 | convolution fusion | flops 284164096 | bytes 6651904 | tf_op jit(solution)/shard_map/thd,shd->hts/dot_general | solution.py:73
  196.7 12.1 %multiply_convert_fusion.4 = bf16[4,512,1024]{2,1,0:T(8,128)(2,1)S(1)} fusion(f32[4,512]{1,0:T(4,128)S(1)} %copy-done.103, f32[4,512]{1,0:T(4,128)S(1)} %copy-done.104, f32[4,512]{1,0:T(4,128)S(1)} %copy-done.105, f32[4,512]{1,0:T(4,128)S(1)} %copy-done.106, f32[4,512]{1,0:T(4,128)S(1)} %copy-done.107, f32[4,512]{1,0:T(4,128)S(1)} %copy-done.108, ...), kind=kOutput, calls=%fused_computation.30 | convolution fusion | flops 568328192 | bytes 12681216 | tf_op jit(solution)/shard_map/thd,shd->hts/dot_general | solution.py:80
  208.9 11.5 %multiply_convert_fusion.5 = bf16[4,512,1024]{2,1,0:T(8,128)(2,1)S(1)} fusion(f32[4,512]{1,0:T(4,128)S(1)} %copy-done.103, f32[4,512]{1,0:T(4,128)S(1)} %copy-done.104, f32[4,512]{1,0:T(4,128)S(1)} %copy-done.105, f32[4,512]{1,0:T(4,128)S(1)} %copy-done.106, f32[4,512]{1,0:T(4,128)S(1)} %copy-done.107, f32[4,512]{1,0:T(4,128)S(1)} %copy-done.108, ...), kind=kOutput, calls=%fused_computation.31 | convolution fusion | flops 568328192 | bytes 12681216 | tf_op jit(solution)/shard_map/thd,shd->hts/dot_general | solution.py:73
  226.9 9.5 %fusion.37 = f32[2,4,128,128]{3,0,2,1:T(2,128)S(1)} fusion(f32[32,4,128,128]{3,2,1,0:T(8,128)S(1)} %fusion.28, f32[32,21,4]{0,1,2:T(8,128)S(1)} %convolution_multiply_fusion), kind=kOutput, calls=%fused_computation.124 | convolution fusion | flops 50331648 | bytes 8916992 | tf_op jit(solution)/shard_map/cjh,chde->jhde/dot_general | solution.py:113
  239.0 19.7 %multiply_convert_fusion.2 = bf16[4,512,1536]{2,1,0:T(8,128)(2,1)S(1)} fusion(bf16[512,4,128]{0,2,1:T(8,128)(2,1)S(1)} %bitcast.304, f32[4,512]{1,0:T(4,128)S(1)} %get-tuple-element.33, f32[4,512]{1,0:T(4,128)S(1)} %get-tuple-element.34, f32[4,512]{1,0:T(4,128)S(1)} %get-tuple-element.35, f32[4,512]{1,0:T(4,128)S(1)} %get-tuple-element.36, ...), kind=kOutput, calls=%fused_computation.14 | convolution fusion | flops 852492288 | bytes 18710528 | tf_op jit(solution)/shard_map/thd,shd->hts/dot_general | solution.py:80
  258.9 18.2 %multiply_convert_fusion.3 = bf16[4,512,1536]{2,1,0:T(8,128)(2,1)S(1)} fusion(bf16[512,4,128]{0,2,1:T(8,128)(2,1)S(1)} %bitcast.311, bf16[1536,4,128]{0,2,1:T(8,128)(2,1)S(1)} %copy-done.44, f32[4,512]{1,0:T(4,128)S(1)} %get-tuple-element.33, f32[4,512]{1,0:T(4,128)S(1)} %get-tuple-element.34, f32[4,512]{1,0:T(4,128)S(1)} %get-tuple-element.35, ...), kind=kOutput, calls=%fused_computation.15 | convolution fusion | flops 852492288 | bytes 18710528 | tf_op jit(solution)/shard_map/thd,shd->hts/dot_general | solution.py:73
  283.7 26.3 %multiply_convert_fusion.1 = bf16[4,512,2048]{2,1,0:T(8,128)(2,1)S(1)} fusion(f32[4,512]{1,0:T(4,128)S(1)} %copy-done.89, f32[4,512]{1,0:T(4,128)S(1)} %copy-done.90, f32[4,512]{1,0:T(4,128)S(1)} %copy-done.91, f32[4,512]{1,0:T(4,128)S(1)} %copy-done.92, f32[4,512]{1,0:T(4,128)S(1)} %copy-done.93, f32[4,512]{1,0:T(4,128)S(1)} %copy-done.94, ...), kind=kOutput, calls=%fused_computation.12 | convolution fusion | flops 1136656384 | bytes 24739840 | tf_op jit(solution)/shard_map/thd,shd->hts/dot_general | solution.py:73
  316.7 5.4 copy.213
  322.1 25.2 %multiply_convert_fusion = bf16[4,512,2048]{2,1,0:T(8,128)(2,1)S(1)} fusion(f32[4,512]{1,0:T(4,128)S(1)} %copy-done.89, f32[4,512]{1,0:T(4,128)S(1)} %copy-done.90, f32[4,512]{1,0:T(4,128)S(1)} %copy-done.91, f32[4,512]{1,0:T(4,128)S(1)} %copy-done.92, f32[4,512]{1,0:T(4,128)S(1)} %copy-done.93, f32[4,512]{1,0:T(4,128)S(1)} %copy-done.94, ...), kind=kOutput, calls=%fused_computation.11 | convolution fusion | flops 1136656384 | bytes 24739840 | tf_op jit(solution)/shard_map/thd,shd->hts/dot_general | solution.py:80
  353.8 5.8 %copy.240 = f32[2048,512]{1,0:T(8,128)} copy(f32[2048,512]{0,1:T(8,128)} %pad_maximum_fusion.1) | data formatting | bytes 8388608 | tf_op jit(solution)/shard_map/concatenate | solution.py:101
  359.6 5.1 convolution_bitcast_fusion.3
  364.7 6.8 %convolution_bitcast_fusion.1 = f32[1536,4,128]{2,0,1:T(8,128)} fusion(bf16[4,512,1536]{2,1,0:T(8,128)(2,1)} %copy-done.25, bf16[512,4,128]{0,2,1:T(8,128)(2,1)S(1)} %bitcast.312), kind=kOutput, calls=%fused_computation.77 | convolution fusion | flops 805306368 | bytes 9961472 | tf_op jit(solution)/shard_map/hts,thd->shd/dot_general | solution.py:89
  374.6 7.2 %convert_bitcast_fusion = bf16[32,4,128,128]{3,0,2,1:T(8,128)(2,1)S(1)} fusion(f32[2,4,128,128]{3,0,2,1:T(2,128)S(1)} %fusion.40, f32[32,21,4]{0,1,2:T(8,128)S(1)} %copy-done.88), kind=kOutput, calls=%fused_computation.55 | convolution fusion | flops 52428800 | bytes 4722688 | tf_op jit(solution)/shard_map/cjh,jhde->chde/dot_general | solution.py:134
  381.8 4.6 fusion.22
  386.4 5.5 %copy.243 = f32[32,64,4,128]{3,2,1,0:T(4,128)} copy(f32[32,64,4,128]{3,1,2,0:T(8,128)S(1)} %fusion.22) | data formatting | bytes 8388608 | tf_op jit(solution)/shard_map/cthe,chde->cthd/transpose | solution.py:141
  391.9 5.5 reshape.1375
  397.4 5.5 %add_convert_fusion = bf16[4,512,512]{2,1,0:T(8,128)(2,1)} fusion(f32[4,512,512]{2,1,0:T(8,128)} %bitcast.280, f32[4,512,512]{2,1,0:T(8,128)} %reshape.1375), kind=kLoop, calls=%fused_computation.52 | loop fusion | flops 2097152 | bytes 10485760 | tf_op jit(solution)/shard_map/convert_element_type | solution.py:152
  402.9 4.7 all-to-all-start.5
  410.2 8.6 %fusion.69 = f32[4,2048,128]{2,1,0:T(8,128)} fusion(bf16[4,512,2048]{2,1,0:T(8,128)(2,1)} %copy-done.20, bf16[512,4,128]{0,2,1:T(8,128)(2,1)} %bitcast.307), kind=kOutput, calls=%fused_computation.247 | convolution fusion | flops 1073741824 | bytes 13107200 | tf_op jit(solution)/shard_map/hts,thd->shd/dot_general | solution.py:89
  422.9 5.4 fusion.3
  428.3 10.7 %copy.256 = bf16[2048,4,128]{2,1,0:T(4,128)(2,1)} copy(bf16[2048,4,128]{2,0,1:T(8,128)(2,1)S(1)} %fusion.3) | data formatting | bytes 4194304 | tf_op jit(solution)/shard_map/convert_element_type | solution.py:153
  443.1 4.9 all-to-all-start.6
  450.7 5.4 convolution_bitcast_fusion.2
  456.0 4.3 fusion.19
  460.3 5.6 %copy.227 = f32[32,64,4,128]{3,2,1,0:T(4,128)} copy(f32[32,64,4,128]{3,1,2,0:T(8,128)S(1)} %fusion.19) | data formatting | bytes 8388608 | tf_op jit(solution)/shard_map/cthd,chde->cthe/transpose | solution.py:138
  465.9 5.5 reshape.1374
  471.4 5.5 %add_convert_fusion.1 = bf16[4,512,512]{2,1,0:T(8,128)(2,1)} fusion(f32[4,512,512]{2,1,0:T(8,128)} %bitcast.279, f32[4,512,512]{2,1,0:T(8,128)} %reshape.1374), kind=kLoop, calls=%fused_computation.54 | loop fusion | flops 2097152 | bytes 10485760 | tf_op jit(solution)/shard_map/convert_element_type | solution.py:151
  476.9 4.7 all-to-all-start.4
  481.6 5.2 convolution_bitcast_fusion
  486.9 6.6 %fusion.70 = f32[4,2048,128]{2,1,0:T(8,128)S(1)} fusion(bf16[4,512,2048]{2,1,0:T(8,128)(2,1)} %copy-done.19, bf16[512,4,128]{0,2,1:T(8,128)(2,1)S(1)} %bitcast.302), kind=kOutput, calls=%fused_computation.248 | convolution fusion | flops 1073741824 | bytes 13107200 | tf_op jit(solution)/shard_map/hts,thd->shd/dot_general | solution.py:95
  494.9 9.8 %copy.268 = bf16[2048,4,128]{2,1,0:T(4,128)(2,1)S(1)} copy(bf16[2048,4,128]{2,0,1:T(8,128)(2,1)S(1)} %fusion.2) | data formatting | bytes 4194304 | tf_op jit(solution)/shard_map/convert_element_type | solution.py:154
  510.9 4.1 copy.244
  519.0 4.1 copy.257
  527.0 4.1 copy.228
  (350 shorter events, 144.7 us)
Async XLA Ops:
  7.2 53.9 %copy-start = (f32[8,21,4]{1,2,0:T(4,128)S(1)}, f32[8,21,4]{1,2,0:T(4,128)}, u32[]{:S(2)}) copy-start(f32[8,21,4]{1,2,0:T(4,128)} %param.10) | copy-start | bytes 8068
  11.1 29.9 %all-to-all-start = ((bf16[512,4,512]{0,2,1:T(8,128)(2,1)}), bf16[512,4,512]{0,2,1:T(8,128)(2,1)S(1)}, u32[]{:S(2)}, u32[]{:S(2)}) async-start(bf16[512,4,512]{0,2,1:T(8,128)(2,1)} %bitcast.284), calls=%async_computation | async-start | bytes 4194304 | tf_op jit(solution)/shard_map/all_to_all | solution.py:30
  42.3 29.3 %all-to-all-start.1 = ((bf16[512,4,512]{0,2,1:T(8,128)(2,1)}), bf16[512,4,512]{0,2,1:T(8,128)(2,1)S(1)}, u32[]{:S(2)}, u32[]{:S(2)}) async-start(bf16[512,4,512]{0,2,1:T(8,128)(2,1)} %bitcast.283), calls=%async_computation.1 | async-start | bytes 4194304 | tf_op jit(solution)/shard_map/all_to_all | solution.py:31
  46.0 15.1 %copy-start.132 = (s32[32]{0:T(128)S(1)}, s32[32]{0:T(128)}, u32[]{:S(2)}) copy-start(s32[32]{0:T(128)} %param.11) | copy-start | bytes 388
  61.3 165.5 %copy-start.87 = (f32[32,21,4]{0,1,2:T(8,128)}, f32[32,21,4]{0,1,2:T(8,128)S(1)}, u32[]{:S(2)}) copy-start(f32[32,21,4]{0,1,2:T(8,128)S(1)} %convolution_multiply_fusion) | copy-start | bytes 32260
  71.6 30.2 %all-to-all-start.2 = ((bf16[512,4,512]{2,0,1:T(8,128)(2,1)}), bf16[512,4,512]{2,0,1:T(8,128)(2,1)}, u32[]{:S(2)}, u32[]{:S(2)}) async-start(bf16[512,4,512]{2,0,1:T(8,128)(2,1)} %bitcast.282), calls=%async_computation.2 | async-start | bytes 4194304 | tf_op jit(solution)/shard_map/all_to_all | solution.py:32
  101.8 32.5 %all-to-all-start.3 = ((bf16[512,4,512]{0,2,1:T(8,128)(2,1)}), bf16[512,4,512]{0,2,1:T(8,128)(2,1)}, u32[]{:S(2)}, u32[]{:S(2)}) async-start(bf16[512,4,512]{0,2,1:T(8,128)(2,1)} %bitcast.281), calls=%async_computation.3 | async-start | bytes 4194304 | tf_op jit(solution)/shard_map/all_to_all | solution.py:33
  106.3 265.2 %all-gather.2.cloned.1.call-start = ((), (), s32[]{:S(2)}) async-start(), calls=%async_computation.8 | async-start | bytes 3932160 | tf_op jit(solution)/shard_map/all_gather | solution.py:116
  149.9 12.9 %copy-start.4 = (bf16[2048,4,128]{2,1,0:T(4,128)(2,1)}, bf16[2048,4,128]{2,1,0:T(4,128)(2,1)S(1)}, u32[]{:S(2)}) copy-start(bf16[2048,4,128]{2,1,0:T(4,128)(2,1)S(1)} %reshape.1371) | copy-start | bytes 6291460
  172.4 63.9 %copy-start.6 = (bf16[2048,4,128]{0,2,1:T(8,128)(2,1)}, bf16[2048,4,128]{0,2,1:T(8,128)(2,1)S(1)}, u32[]{:S(2)}) copy-start(bf16[2048,4,128]{0,2,1:T(8,128)(2,1)S(1)} %copy.313) | copy-start | bytes 6291460
  176.8 8.4 %copy-start.39 = (bf16[1,512,512]{1,2,0:T(8,128)(2,1)S(1)}, bf16[1,512,512]{1,2,0:T(8,128)(2,1)}, u32[]{:S(2)}) copy-start(bf16[1,512,512]{1,2,0:T(8,128)(2,1)} %get-tuple-element.16) | copy-start | bytes 1572868
  176.8 8.4 %copy-start.75 = (pred[512,512]{1,0:T(8,128)(4,1)S(1)}, pred[512,512]{1,0:T(8,128)(4,1)}, u32[]{:S(2)}) copy-start(pred[512,512]{1,0:T(8,128)(4,1)} %get-tuple-element.95) | copy-start | bytes 786436
  176.8 8.4 %copy-start.76 = (pred[512,512]{1,0:T(8,128)(4,1)S(1)}, pred[512,512]{1,0:T(8,128)(4,1)}, u32[]{:S(2)}) copy-start(pred[512,512]{1,0:T(8,128)(4,1)} %get-tuple-element.96) | copy-start | bytes 786436
  185.4 8.6 %copy-start.34 = (bf16[1,512,512]{1,2,0:T(8,128)(2,1)S(1)}, bf16[1,512,512]{1,2,0:T(8,128)(2,1)}, u32[]{:S(2)}) copy-start(bf16[1,512,512]{1,2,0:T(8,128)(2,1)} %copy.200) | copy-start | bytes 1572868
  185.4 10.4 %copy-start.109 = (f32[4,512]{1,0:T(4,128)S(1)}, f32[4,512]{1,0:T(4,128)}, u32[]{:S(2)}) copy-start(f32[4,512]{1,0:T(4,128)} %get-tuple-element.52) | copy-start | bytes 24580
  185.4 10.4 %copy-start.110 = (f32[4,512]{1,0:T(4,128)S(1)}, f32[4,512]{1,0:T(4,128)}, u32[]{:S(2)}) copy-start(f32[4,512]{1,0:T(4,128)} %get-tuple-element.53) | copy-start | bytes 24580
  185.5 10.4 %copy-start.111 = (f32[4,512]{1,0:T(4,128)S(1)}, f32[4,512]{1,0:T(4,128)}, u32[]{:S(2)}) copy-start(f32[4,512]{1,0:T(4,128)} %get-tuple-element.54) | copy-start | bytes 24580
  196.7 12.2 %copy-start.27 = (bf16[1024,4,128]{0,2,1:T(8,128)(2,1)S(1)}, bf16[1024,4,128]{0,2,1:T(8,128)(2,1)}, u32[]{:S(2)}) copy-start(bf16[1024,4,128]{0,2,1:T(8,128)(2,1)} %reshape.1383) | copy-start | bytes 3145732
  196.7 12.2 %copy-start.42 = (bf16[1,512,512]{1,2,0:T(8,128)(2,1)S(1)}, bf16[1,512,512]{1,2,0:T(8,128)(2,1)}, u32[]{:S(2)}) copy-start(bf16[1,512,512]{1,2,0:T(8,128)(2,1)} %get-tuple-element.19) | copy-start | bytes 1572868
  196.7 12.2 %copy-start.112 = (f32[4,512]{1,0:T(4,128)S(1)}, f32[4,512]{1,0:T(4,128)}, u32[]{:S(2)}) copy-start(f32[4,512]{1,0:T(4,128)} %get-tuple-element.55) | copy-start | bytes 24580
  196.7 12.2 %copy-start.113 = (f32[4,512]{1,0:T(4,128)S(1)}, f32[4,512]{1,0:T(4,128)}, u32[]{:S(2)}) copy-start(f32[4,512]{1,0:T(4,128)} %get-tuple-element.56) | copy-start | bytes 24580
  196.7 12.2 %copy-start.114 = (f32[4,512]{1,0:T(4,128)S(1)}, f32[4,512]{1,0:T(4,128)}, u32[]{:S(2)}) copy-start(f32[4,512]{1,0:T(4,128)} %get-tuple-element.57) | copy-start | bytes 24580
  208.8 11.6 %copy-start.15 = (bf16[4,512,1024]{2,1,0:T(8,128)(2,1)}, bf16[4,512,1024]{2,1,0:T(8,128)(2,1)S(1)}, u32[]{:S(2)}) copy-start(bf16[4,512,1024]{2,1,0:T(8,128)(2,1)S(1)} %multiply_convert_fusion.4) | copy-start | bytes 12582916
  226.8 9.5 %copy-start.21 = (bf16[2048,4,128]{0,2,1:T(8,128)(2,1)S(1)}, bf16[2048,4,128]{0,2,1:T(8,128)(2,1)}, u32[]{:S(2)}) copy-start(bf16[2048,4,128]{0,2,1:T(8,128)(2,1)} %copy.214) | copy-start | bytes 6291460
  238.9 19.9 %copy-start.40 = (bf16[1,512,512]{1,2,0:T(8,128)(2,1)S(1)}, bf16[1,512,512]{1,2,0:T(8,128)(2,1)}, u32[]{:S(2)}) copy-start(bf16[1,512,512]{1,2,0:T(8,128)(2,1)} %get-tuple-element.18) | copy-start | bytes 1572868
  238.9 19.9 %copy-start.44 = (bf16[1536,4,128]{0,2,1:T(8,128)(2,1)S(1)}, bf16[1536,4,128]{0,2,1:T(8,128)(2,1)}, u32[]{:S(2)}) copy-start(bf16[1536,4,128]{0,2,1:T(8,128)(2,1)} %reshape.1384) | copy-start | bytes 4718596
  238.9 19.9 %copy-start.50 = (pred[512,1536]{1,0:T(8,128)(4,1)S(1)}, pred[512,1536]{1,0:T(8,128)(4,1)}, u32[]{:S(2)}) copy-start(pred[512,1536]{1,0:T(8,128)(4,1)} %get-tuple-element.68) | copy-start | bytes 2359300
  238.9 19.9 %copy-start.51 = (pred[512,1536]{1,0:T(8,128)(4,1)S(1)}, pred[512,1536]{1,0:T(8,128)(4,1)}, u32[]{:S(2)}) copy-start(pred[512,1536]{1,0:T(8,128)(4,1)} %get-tuple-element.69) | copy-start | bytes 2359300
  238.9 19.9 %copy-start.52 = (pred[512,1536]{1,0:T(8,128)(4,1)S(1)}, pred[512,1536]{1,0:T(8,128)(4,1)}, u32[]{:S(2)}) copy-start(pred[512,1536]{1,0:T(8,128)(4,1)} %get-tuple-element.70) | copy-start | bytes 2359300
  238.9 19.9 %copy-start.53 = (pred[512,1536]{1,0:T(8,128)(4,1)S(1)}, pred[512,1536]{1,0:T(8,128)(4,1)}, u32[]{:S(2)}) copy-start(pred[512,1536]{1,0:T(8,128)(4,1)} %get-tuple-element.71) | copy-start | bytes 2359300
  238.9 19.9 %copy-start.54 = (pred[512,1536]{1,0:T(8,128)(4,1)S(1)}, pred[512,1536]{1,0:T(8,128)(4,1)}, u32[]{:S(2)}) copy-start(pred[512,1536]{1,0:T(8,128)(4,1)} %get-tuple-element.72) | copy-start | bytes 2359300
  238.9 19.9 %copy-start.55 = (pred[512,1536]{1,0:T(8,128)(4,1)S(1)}, pred[512,1536]{1,0:T(8,128)(4,1)}, u32[]{:S(2)}) copy-start(pred[512,1536]{1,0:T(8,128)(4,1)} %get-tuple-element.73) | copy-start | bytes 2359300
  239.0 19.9 %copy-start.56 = (pred[512,1536]{1,0:T(8,128)(4,1)S(1)}, pred[512,1536]{1,0:T(8,128)(4,1)}, u32[]{:S(2)}) copy-start(pred[512,1536]{1,0:T(8,128)(4,1)} %get-tuple-element.74) | copy-start | bytes 2359300
  239.0 19.9 %copy-start.57 = (pred[512,1536]{1,0:T(8,128)(4,1)S(1)}, pred[512,1536]{1,0:T(8,128)(4,1)}, u32[]{:S(2)}) copy-start(pred[512,1536]{1,0:T(8,128)(4,1)} %get-tuple-element.75) | copy-start | bytes 2359300
  239.0 19.9 %copy-start.58 = (pred[512,1536]{1,0:T(8,128)(4,1)S(1)}, pred[512,1536]{1,0:T(8,128)(4,1)}, u32[]{:S(2)}) copy-start(pred[512,1536]{1,0:T(8,128)(4,1)} %get-tuple-element.76) | copy-start | bytes 2359300
  239.0 19.9 %copy-start.59 = (pred[512,1536]{1,0:T(8,128)(4,1)S(1)}, pred[512,1536]{1,0:T(8,128)(4,1)}, u32[]{:S(2)}) copy-start(pred[512,1536]{1,0:T(8,128)(4,1)} %get-tuple-element.77) | copy-start | bytes 2359300
  239.0 19.9 %copy-start.60 = (pred[512,1536]{1,0:T(8,128)(4,1)S(1)}, pred[512,1536]{1,0:T(8,128)(4,1)}, u32[]{:S(2)}) copy-start(pred[512,1536]{1,0:T(8,128)(4,1)} %get-tuple-element.78) | copy-start | bytes 2359300
  239.0 19.9 %copy-start.61 = (pred[512,1536]{1,0:T(8,128)(4,1)S(1)}, pred[512,1536]{1,0:T(8,128)(4,1)}, u32[]{:S(2)}) copy-start(pred[512,1536]{1,0:T(8,128)(4,1)} %get-tuple-element.79) | copy-start | bytes 2359300
  258.8 18.3 %copy-start.25 = (bf16[4,512,1536]{2,1,0:T(8,128)(2,1)}, bf16[4,512,1536]{2,1,0:T(8,128)(2,1)S(1)}, u32[]{:S(2)}) copy-start(bf16[4,512,1536]{2,1,0:T(8,128)(2,1)S(1)} %multiply_convert_fusion.2) | copy-start | bytes 18874372
  283.7 26.4 %copy-start.7 = (bf16[2048,4,128]{0,2,1:T(8,128)(2,1)S(1)}, bf16[2048,4,128]{0,2,1:T(8,128)(2,1)}, u32[]{:S(2)}) copy-start(bf16[2048,4,128]{0,2,1:T(8,128)(2,1)} %copy-done.6) | copy-start | bytes 6291460
  322.1 25.3 %copy-start.22 = (bf16[2048,4,128]{0,2,1:T(8,128)(2,1)S(1)}, bf16[2048,4,128]{0,2,1:T(8,128)(2,1)}, u32[]{:S(2)}) copy-start(bf16[2048,4,128]{0,2,1:T(8,128)(2,1)} %copy.214) | copy-start | bytes 6291460
  364.7 9.8 %copy-start.88 = (f32[32,21,4]{0,1,2:T(8,128)S(1)}, f32[32,21,4]{0,1,2:T(8,128)}, u32[]{:S(2)}) copy-start(f32[32,21,4]{0,1,2:T(8,128)} %copy-done.87) | copy-start | bytes 32260
  372.9 8.9 %copy-start.13 = (bf16[32,64,4,128]{3,2,1,0:T(4,128)(2,1)S(1)}, bf16[32,64,4,128]{3,2,1,0:T(4,128)(2,1)}, u32[]{:S(2)}) copy-start(bf16[32,64,4,128]{3,2,1,0:T(4,128)(2,1)} %reshape_reshape.7) | copy-start | bytes 6291460
  402.9 40.2 %all-to-all-start.5 = ((bf16[4,512,512]{2,1,0:T(8,128)(2,1)}), bf16[4,512,512]{2,1,0:T(8,128)(2,1)}, u32[]{:S(2)}, u32[]{:S(2)}) async-start(bf16[4,512,512]{2,1,0:T(8,128)(2,1)} %add_convert_fusion), calls=%async_computation.5 | async-start | bytes 4194304 | tf_op jit(solution)/shard_map/all_to_all | solution.py:157
  410.2 8.6 %copy-start.32 = (f32[12,4,128,128]{3,2,1,0:T(8,128)S(1)}, f32[12,4,128,128]{3,2,1,0:T(8,128)}, u32[]{:S(2)}) copy-start(f32[12,4,128,128]{3,2,1,0:T(8,128)} %all-gather.2.cloned.1.call-done) | copy-start | bytes 9437188
  443.1 33.7 %all-to-all-start.6 = ((bf16[4,512,512]{2,1,0:T(8,128)(2,1)}), bf16[4,512,512]{2,1,0:T(8,128)(2,1)}, u32[]{:S(2)}, u32[]{:S(2)}) async-start(bf16[4,512,512]{2,1,0:T(8,128)(2,1)} %all_to_all.118), calls=%async_computation.6 | async-start | bytes 4194304 | tf_op jit(solution)/shard_map/all_to_all | solution.py:158
  476.9 30.4 %all-to-all-start.4 = ((bf16[4,512,512]{2,1,0:T(8,128)(2,1)}), bf16[4,512,512]{2,1,0:T(8,128)(2,1)}, u32[]{:S(2)}, u32[]{:S(2)}) async-start(bf16[4,512,512]{2,1,0:T(8,128)(2,1)} %add_convert_fusion.1), calls=%async_computation.4 | async-start | bytes 4194304 | tf_op jit(solution)/shard_map/all_to_all | solution.py:156
  507.3 29.3 %all-to-all-start.7 = ((bf16[4,512,512]{2,1,0:T(8,128)(2,1)}), bf16[4,512,512]{2,1,0:T(8,128)(2,1)S(1)}, u32[]{:S(2)}, u32[]{:S(2)}) async-start(bf16[4,512,512]{2,1,0:T(8,128)(2,1)} %all_to_all.122), calls=%async_computation.7 | async-start | bytes 4194304 | tf_op jit(solution)/shard_map/all_to_all | solution.py:159
  (94 other events, 477.5 us)
Sparse Core Ops, SparseCore 0:
  239.0 66.0 all-gather.1
where the time goes:
time: 559 us; the launch traced here: 550 us
  matrix products  231 us (41%)
  local copies, waits for them, and re-layouts  177 us (32%)
  other arithmetic  56.1 us (10%)
  starting transfers between devices  35.2 us (6%)
  waiting for transfers between devices  33.6 us (6%)
  between operations  16.2 us (3%)
    dot_general x4, matrix products, shards(): jnp.einsum('thd,shd->hts', grad_block, value_part, preferred_element_type...  65.2 us
    dot_general x4, matrix products, shards(): jnp.einsum('thd,shd->hts', query_block, key_part, preferred_element_type=...  62.6 us
    le x4, other arithmetic, shards(): col_pos[None, :] <= row_pos[:, None]  38.2 us
    unnamed x273, local copies, waits for them, and re-layouts  32.9 us
    dot_general x4, matrix products, shards(): jnp.einsum('hts,thd->shd', score_grads, query_block, preferred_element_ty...  23.1 us
    dot_general x4, matrix products, shards(): jnp.einsum('hts,thd->shd', attn_weights, grad_block, preferred_element_ty...  19.8 us
    all_to_all x1, waiting for transfers between devices, shards(): lax.all_to_all(values, 'head', split_axis=1, concat_axis=0, tiled=True)  19.5 us
    slice x7, local copies, waits for them, and re-layouts, shards(): key_part = key_heads[:finish]  17.1 us
  transfers between devices with their start and end apart: 9, of which 5 were waited for; matrix products, arithmetic and copies ran while one was open for 56% of the time, Pallas kernels for 0%

commit v1 on v0

--- a/solution.py
+++ b/solution.py
@@ -5,6 +5,22 @@
 from jax.sharding import PartitionSpec as P
 
 HIGHEST = lax.Precision.HIGHEST
+
+
+def pairwise_exchange(x, axis, split, join):
+    ways, here = (lax.axis_size(axis), lax.axis_index(axis))
+    width = x.shape[split] // ways
+    shape = list(x.shape)
+    shape[split] = width
+    height = shape[join]
+    shape[join] = height * ways
+    full = jnp.zeros(shape, x.dtype)
+    for mask in range(ways):
+        part = lax.dynamic_slice_in_dim(x, (here ^ mask) * width, width, axis=split)
+        if mask:
+            part = lax.ppermute(part, axis, [(d, d ^ mask) for d in range(ways)])
+        full = lax.dynamic_update_slice_in_dim(full, part, (here ^ mask) * height, axis=join)
+    return full
 
 
 def level_of(xor_value, limit):
@@ -29,7 +45,7 @@
     query_flat, key_flat, value_flat, grad_flat = (
         lax.all_to_all(queries, "head", split_axis=1, concat_axis=0, tiled=True),
         lax.all_to_all(keys, "head", split_axis=1, concat_axis=0, tiled=True),
-        lax.all_to_all(values, "head", split_axis=1, concat_axis=0, tiled=True),
+        pairwise_exchange(values, "head", 1, 0),
         lax.all_to_all(out_grad, "head", split_axis=1, concat_axis=0, tiled=True),
     )
     heads_here = level_table.shape[2]

time: 559 us -> 542 us (0.970)
  waiting for transfers between devices: 33.6 us -> 19.9 us
  local copies, waits for them, and re-layouts: 177 us -> 167 us
  matrix products: 231 us -> 238 us
    all_to_all x1 -> x0, waiting for transfers between devices: 19.5 us -> none  [shards(): lax.all_to_all(values, 'head', split_axis=1, concat_axis=0, tiled=True)]
    all_to_all x1, waiting for transfers between devices: 0.84 us -> 12.8 us  [shards(): lax.all_to_all(keys, 'head', split_axis=1, concat_axis=0, tiled=True)]
    all_to_all x1, waiting for transfers between devices: 11.2 us -> 0.01 us  [shards(): lax.all_to_all(queries, 'head', split_axis=1, concat_axis=0, tiled=True)]
    dot_general x4, matrix products: 10.4 us -> 20.5 us  [shards(): jnp.einsum('hts,shd->thd', score_grads, key_part, preferred_element_type=...]
    slice x7 -> x3, local copies, waits for them, and re-layouts: 12.6 us -> 3.31 us  [shards(): value_part = value_heads[:finish]]
    slice x7, local copies, waits for them, and re-layouts: 17.1 us -> 8.47 us  [shards(): key_part = key_heads[:finish]]
    unnamed x273 -> x269, local copies, waits for them, and re-layouts: 32.9 us -> 40.4 us
    reshape x2 -> x0, local copies, waits for them, and re-layouts: 6.94 us -> none  [shards(): value_heads = value_flat.reshape(head_shape)]
  transfers between devices with their start and end apart: 9 -> 11, of which waited for: 5 -> 3; matrix products, arithmetic and copies ran while one was open for 56% -> 51% of each run, Pallas kernels for 0% -> 0%
where the time goes in v1:
time: 542 us; the launch traced here: 532 us
  matrix products  238 us (44%)
  local copies, waits for them, and re-layouts  167 us (31%)
  other arithmetic  58 us (11%)
  starting transfers between devices  33.2 us (6%)
  waiting for transfers between devices  19.9 us (4%)
  between operations  16.2 us (3%)
    dot_general x4, matrix products, shards(): jnp.einsum('thd,shd->hts', grad_block, value_part, preferred_element_type...  68.2 us
    dot_general x4, matrix products, shards(): jnp.einsum('thd,shd->hts', query_block, key_part, preferred_element_type=...  61.5 us
    unnamed x269, local copies, waits for them, and re-layouts  40.4 us
    le x4, other arithmetic, shards(): col_pos[None, :] <= row_pos[:, None]  38.1 us
    dot_general x4, matrix products, shards(): jnp.einsum('hts,shd->thd', score_grads, key_part, preferred_element_type=...  20.5 us
    dot_general x4, matrix products, shards(): jnp.einsum('hts,thd->shd', score_grads, query_block, preferred_element_ty...  19.5 us
    dot_general x4, matrix products, shards(): jnp.einsum('hts,thd->shd', attn_weights, grad_block, preferred_element_ty...  16.5 us
    all_to_all x1, waiting for transfers between devices, shards(): lax.all_to_all(keys, 'head', split_axis=1, concat_axis=0, tiled=True)  12.8 us
  transfers between devices with their start and end apart: 11, of which 3 were waited for; matrix products, arithmetic and copies ran while one was open for 51% of the time, Pallas kernels for 0%

profile of v1, /device:TPU:0, one launch (start us, length us, event | category | flops | bytes accessed | tf_op | source)
XLA Modules:
  0.0 532.4 jit_solution(6454778944967921700)
XLA Ops:
  11.1 4.2 all-to-all-start
  25.6 15.1 %iota_compare_fusion = (pred[512,2048]{1,0:T(8,128)(4,1)}, pred[512,2048]{1,0:T(8,128)(4,1)}, pred[512,2048]{1,0:T(8,128)(4,1)}, pred[512,2048]{1,0:T(8,128)(4,1...) fusion(s32[512]{0:T(512)S(1)} %iota_add_fusion.2), kind=kLoop, calls=%fused_computation.73 | loop fusion | flops 48234496 | bytes 13633536 | tf_op jit(solution)/shard_map/le | solution.py:88
  40.7 10.5 %broadcast_compare_fusion.24 = (pred[512,1536]{1,0:T(8,128)(4,1)}, pred[512,1536]{1,0:T(8,128)(4,1)}, pred[512,1536]{1,0:T(8,128)(4,1)}, pred[512,1536]{1,0:T(8,...) fusion(s32[1536]{0:T(1024)S(1)} %iota_add_fusion, ...), kind=kLoop, calls=%fused_computation.119 | loop fusion | flops 36175872 | bytes 10231808 | tf_op jit(solution)/shard_map/le | solution.py:88
  58.7 4.2 broadcast_compare_fusion.50
  72.8 8.3 %broadcast_compare_fusion.37 = (pred[512,1024]{1,0:T(8,128)(4,1)}, pred[512,1024]{1,0:T(8,128)(4,1)}, pred[512,1024]{1,0:T(8,128)(4,1)}, pred[512,1024]{1,0:T(8,...) fusion(s32[1024]{0:T(1024)S(1)} %iota_add_fusion.1, ...), kind=kLoop, calls=%fused_computation.146 | loop fusion | flops 24117248 | bytes 6821888 | tf_op jit(solution)/shard_map/le | solution.py:88
  81.1 12.8 %all-to-all-done.1 = bf16[512,4,512]{0,2,1:T(8,128)(2,1)S(1)} async-done(((bf16[512,4,512]{0,2,1:T(8,128)(2,1)}), bf16[512,4,512]{0,2,1:T(8,128)(2,1)S(1)}, u32[]{:S(2)}, u32[]{:S(2)}) %all-to-all-start.1) | async-done | bytes 2097184 | tf_op jit(solution)/shard_map/all_to_all | solution.py:47
  93.9 4.5 all-to-all-start.2
  112.9 4.3 copy.220
  118.6 5.5 %all-to-all-done.2 = bf16[512,4,512]{0,2,1:T(8,128)(2,1)} async-done(((bf16[512,4,512]{0,2,1:T(8,128)(2,1)}), bf16[512,4,512]{0,2,1:T(8,128)(2,1)}, u32[]{:S(2)}, u32[]{:S(2)}) %all-to-all-start.2) | async-done | bytes 2097184 | tf_op jit(solution)/shard_map/all_to_all | solution.py:49
  124.2 4.1 copy.222
  133.3 14.2 %fusion.2 = bf16[4,512,1024]{2,1,0:T(8,128)(2,1)} fusion(f32[4,512]{1,0:T(4,128)S(1)} %get-tuple-element.50, f32[4,512]{1,0:T(4,128)S(1)} %get-tuple-element.51, f32[4,512]{1,0:T(4,128)S(1)} %get-tuple-element.52, f32[4,512]{1,0:T(4,128)S(1)} %get-tuple-element.53, f32[4,512]{1,0:T(4,128)S(1)} %get-tuple-element.54, f32[4,512]{1,0:T(4,128)S(1)} %get-tuple-element.55, ...), kind=kOutput, calls=%fused_computation.31 | convolution fusion | flops 568328192 | bytes 12681216 | tf_op jit(solution)/shard_map/thd,shd->hts/dot_general | solution.py:96
  147.6 11.4 %multiply_convert_fusion.2 = bf16[4,512,1024]{2,1,0:T(8,128)(2,1)S(1)} fusion(f32[4,512]{1,0:T(4,128)S(1)} %get-tuple-element.50, f32[4,512]{1,0:T(4,128)S(1)} %get-tuple-element.51, f32[4,512]{1,0:T(4,128)S(1)} %get-tuple-element.52, f32[4,512]{1,0:T(4,128)S(1)} %get-tuple-element.53, f32[4,512]{1,0:T(4,128)S(1)} %get-tuple-element.54, ...), kind=kOutput, calls=%fused_computation.34 | convolution fusion | flops 568328192 | bytes 12681216 | tf_op jit(solution)/shard_map/thd,shd->hts/dot_general | solution.py:89
  169.3 20.4 %fusion.1 = bf16[4,512,1536]{2,1,0:T(8,128)(2,1)} fusion(bf16[1536,4,128]{0,2,1:T(8,128)(2,1)} %bitcast.309, bf16[512,4,128]{0,2,1:T(8,128)(2,1)} %bitcast.334, f32[4,512]{1,0:T(4,128)S(1)} %get-tuple-element.37, f32[4,512]{1,0:T(4,128)S(1)} %get-tuple-element.38, f32[4,512]{1,0:T(4,128)S(1)} %get-tuple-element.39, f32[4,512]{1,0:T(4,128)S(1)} %get-tuple-element.40, ...), kind=kOutput, calls=%fused_computation.16 | convolution fusion | flops 852492288 | bytes 18710528 | tf_op jit(solution)/shard_map/thd,shd->hts/dot_general | solution.py:96
  189.9 17.0 %multiply_convert_fusion.1 = bf16[4,512,1536]{2,1,0:T(8,128)(2,1)S(1)} fusion(bf16[512,4,128]{0,2,1:T(8,128)(2,1)S(1)} %bitcast.326, bf16[1536,4,128]{0,2,1:T(8,128)(2,1)S(1)} %copy-done.41, f32[4,512]{1,0:T(4,128)S(1)} %get-tuple-element.37, f32[4,512]{1,0:T(4,128)S(1)} %get-tuple-element.38, f32[4,512]{1,0:T(4,128)S(1)} %get-tuple-element.39, ...), kind=kOutput, calls=%fused_computation.17 | convolution fusion | flops 852492288 | bytes 18710528 | tf_op jit(solution)/shard_map/thd,shd->hts/dot_general | solution.py:89
  216.0 4.1 reshape.1368
  228.7 8.8 %fusion.7 = bf16[4,512,512]{2,1,0:T(8,128)(2,1)} fusion(bf16[512,4,128]{0,2,1:T(8,128)(2,1)} %bitcast.322, bf16[512,4,128]{0,2,1:T(8,128)(2,1)} %bitcast.332, f32[4,512]{1,0:T(4,128)S(1)} %copy-done.100, f32[4,512]{1,0:T(4,128)S(1)} %copy-done.101, f32[4,512]{1,0:T(4,128)S(1)} %copy-done.102, f32[4,512]{1,0:T(4,128)S(1)} %copy-done.103, ...), kind=kOutput, calls=%fused_computation.56 | convolution fusion | flops 284164096 | bytes 6651904 | tf_op jit(solution)/shard_map/thd,shd->hts/dot_general | solution.py:96
  237.6 6.9 %multiply_convert_fusion.3 = bf16[4,512,512]{2,1,0:T(8,128)(2,1)S(1)} fusion(bf16[512,4,128]{0,2,1:T(8,128)(2,1)S(1)} %bitcast.328, bf16[512,4,128]{0,2,1:T(8,128)(2,1)S(1)} %bitcast.321, f32[4,512]{1,0:T(4,128)S(1)} %copy-done.100, f32[4,512]{1,0:T(4,128)S(1)} %copy-done.101, f32[4,512]{1,0:T(4,128)S(1)} %copy-done.102, f32[4,512]{1,0:T(4,128)S(1)} %copy-done.103, ...), kind=kOutput, calls=%fused_computation.74 | convolution fusion | flops 284164096 | bytes 6651904 | tf_op jit(solution)/shard_map/thd,shd->hts/dot_general | solution.py:89
  251.5 9.3 %fusion.42 = f32[2,4,128,128]{3,0,2,1:T(2,128)S(1)} fusion(f32[32,4,128,128]{3,2,1,0:T(8,128)S(1)} %fusion.32, f32[32,21,4]{0,1,2:T(8,128)S(1)} %copy-done.98), kind=kOutput, calls=%fused_computation.128 | convolution fusion | flops 50331648 | bytes 8916992 | tf_op jit(solution)/shard_map/cjh,chde->jhde/dot_general | solution.py:129
  262.5 6.5 %fusion.75 = f32[4,512,128]{1,2,0:T(8,128)} fusion(bf16[4,512,1536]{2,1,0:T(8,128)(2,1)} %fusion.1, bf16[1536,4,128]{0,2,1:T(8,128)(2,1)} %reshape.1378), kind=kOutput, calls=%fused_computation.258 | convolution fusion | flops 805306368 | bytes 8912896 | tf_op jit(solution)/shard_map/hts,shd->thd/dot_general | solution.py:101
  269.1 26.2 %multiply_convert_fusion = bf16[4,512,2048]{2,1,0:T(8,128)(2,1)S(1)} fusion(f32[4,512]{1,0:T(4,128)S(1)} %copy-done.109, f32[4,512]{1,0:T(4,128)S(1)} %copy-done.110, f32[4,512]{1,0:T(4,128)S(1)} %copy-done.111, f32[4,512]{1,0:T(4,128)S(1)} %copy-done.112, f32[4,512]{1,0:T(4,128)S(1)} %copy-done.113, f32[4,512]{1,0:T(4,128)S(1)} %copy-done.114, ...), kind=kOutput, calls=%fused_computation.13 | convolution fusion | flops 1136656384 | bytes 24739840 | tf_op jit(solution)/shard_map/thd,shd->hts/dot_general | solution.py:89
  303.1 5.6 %copy.218 = f32[2048,512]{1,0:T(8,128)} copy(f32[2048,512]{0,1:T(8,128)} %pad_maximum_fusion) | data formatting | bytes 8388608 | tf_op jit(solution)/shard_map/concatenate | solution.py:116
  308.9 8.7 %fusion.77 = f32[4,2048,128]{2,1,0:T(8,128)} fusion(bf16[4,512,2048]{2,1,0:T(8,128)(2,1)} %copy-done.2, bf16[512,4,128]{0,2,1:T(8,128)(2,1)} %bitcast.330), kind=kOutput, calls=%fused_computation.260 | convolution fusion | flops 1073741824 | bytes 13107200 | tf_op jit(solution)/shard_map/hts,thd->shd/dot_general | solution.py:111
  317.7 24.8 %fusion = bf16[4,512,2048]{2,1,0:T(8,128)(2,1)} fusion(f32[4,512]{1,0:T(4,128)S(1)} %copy-done.109, f32[4,512]{1,0:T(4,128)S(1)} %copy-done.110, f32[4,512]{1,0:T(4,128)S(1)} %copy-done.111, f32[4,512]{1,0:T(4,128)S(1)} %copy-done.112, f32[4,512]{1,0:T(4,128)S(1)} %copy-done.113, f32[4,512]{1,0:T(4,128)S(1)} %copy-done.114, f32[4,512]{1,0:T(4,128)S(1)} %copy-done.115, ...), kind=kOutput, calls=%fused_computation.12 | convolution fusion | flops 1136656384 | bytes 24739840 | tf_op jit(solution)/shard_map/thd,shd->hts/dot_general | solution.py:96
  345.5 7.4 %convert_bitcast_fusion = bf16[32,4,128,128]{3,0,2,1:T(8,128)(2,1)S(1)} fusion(f32[2,4,128,128]{3,0,2,1:T(2,128)S(1)} %fusion.48, f32[32,21,4]{0,1,2:T(8,128)S(1)} %copy-done.98), kind=kOutput, calls=%fused_computation.59 | convolution fusion | flops 52428800 | bytes 4722688 | tf_op jit(solution)/shard_map/cjh,jhde->chde/dot_general | solution.py:150
  354.9 4.3 fusion.23
  359.2 5.6 %copy.231 = f32[32,64,4,128]{3,2,1,0:T(4,128)} copy(f32[32,64,4,128]{3,1,2,0:T(8,128)S(1)} %fusion.23) | data formatting | bytes 8388608 | tf_op jit(solution)/shard_map/cthd,chde->cthe/transpose | solution.py:154
  364.8 5.5 %reshape.1370 = f32[4,512,512]{2,1,0:T(8,128)} reshape(f32[32,64,4,128]{3,2,1,0:T(4,128)} %copy.231) | data formatting | bytes 8388608 | tf_op jit(solution)/shard_map/reshape | solution.py:156
  370.2 5.5 %add_convert_fusion.1 = bf16[4,512,512]{2,1,0:T(8,128)(2,1)} fusion(f32[4,512,512]{2,1,0:T(8,128)} %bitcast.298, f32[4,512,512]{2,1,0:T(8,128)} %reshape.1370), kind=kLoop, calls=%fused_computation.58 | loop fusion | flops 2097152 | bytes 10485760 | tf_op jit(solution)/shard_map/convert_element_type | solution.py:167
  375.7 4.6 all-to-all-start.3
  383.9 8.0 %fusion.36 = f32[4,512,128]{1,2,0:T(8,128)} fusion(bf16[4,512,2048]{2,1,0:T(8,128)(2,1)} %fusion, bf16[2048,4,128]{2,1,0:T(4,128)(2,1)} %reshape.1368), kind=kOutput, calls=%fused_computation.122 | convolution fusion | flops 1073741824 | bytes 11534336 | tf_op jit(solution)/shard_map/hts,shd->thd/dot_general | solution.py:101
  395.9 5.2 fusion.5
  401.2 10.7 %copy.276 = bf16[2048,4,128]{2,1,0:T(4,128)(2,1)} copy(bf16[2048,4,128]{2,0,1:T(8,128)(2,1)S(1)} %fusion.5) | data formatting | bytes 4194304 | tf_op jit(solution)/shard_map/convert_element_type | solution.py:170
  411.9 4.2 all_to_all.107
  416.1 4.7 all-to-all-start.6
  420.8 4.3 pad_maximum_fusion.1
  425.1 5.5 %copy.248 = f32[2048,512]{1,0:T(8,128)} copy(f32[2048,512]{0,1:T(8,128)} %pad_maximum_fusion.1) | data formatting | bytes 8388608 | tf_op jit(solution)/shard_map/concatenate | solution.py:117
  430.6 5.3 convolution_bitcast_fusion.3
  435.9 4.5 fusion.26
  440.4 5.6 %copy.251 = f32[32,64,4,128]{3,2,1,0:T(4,128)} copy(f32[32,64,4,128]{3,1,2,0:T(8,128)S(1)} %fusion.26) | data formatting | bytes 8388608 | tf_op jit(solution)/shard_map/cthe,chde->cthd/transpose | solution.py:157
  446.0 5.5 %reshape.1371 = f32[4,512,512]{2,1,0:T(8,128)} reshape(f32[32,64,4,128]{3,2,1,0:T(4,128)} %copy.251) | data formatting | bytes 8388608 | tf_op jit(solution)/shard_map/reshape | solution.py:159
  451.5 5.5 %add_convert_fusion = bf16[4,512,512]{2,1,0:T(8,128)(2,1)} fusion(f32[4,512,512]{2,1,0:T(8,128)} %bitcast.299, f32[4,512,512]{2,1,0:T(8,128)} %reshape.1371), kind=kLoop, calls=%fused_computation.57 | loop fusion | flops 2097152 | bytes 10485760 | tf_op jit(solution)/shard_map/convert_element_type | solution.py:168
  457.0 5.0 all-to-all-start.4
  464.5 5.2 convolution_bitcast_fusion.1
  469.7 6.6 %fusion.76 = f32[4,2048,128]{2,1,0:T(8,128)S(1)} fusion(bf16[4,512,2048]{2,1,0:T(8,128)(2,1)} %fusion, bf16[512,4,128]{0,2,1:T(8,128)(2,1)S(1)} %bitcast.325), kind=kOutput, calls=%fused_computation.259 | convolution fusion | flops 1073741824 | bytes 13107200 | tf_op jit(solution)/shard_map/hts,thd->shd/dot_general | solution.py:105
  477.7 9.9 %copy.264 = bf16[2048,4,128]{2,1,0:T(4,128)(2,1)S(1)} copy(bf16[2048,4,128]{2,0,1:T(8,128)(2,1)S(1)} %fusion.6) | data formatting | bytes 4194304 | tf_op jit(solution)/shard_map/convert_element_type | solution.py:169
  493.4 4.1 copy.232
  501.5 4.1 copy.277
  509.5 4.1 copy.252
  (349 shorter events, 137.8 us)
Async XLA Ops:
  7.2 44.1 %copy-start = (f32[8,21,4]{1,2,0:T(4,128)S(1)}, f32[8,21,4]{1,2,0:T(4,128)}, u32[]{:S(2)}) copy-start(f32[8,21,4]{1,2,0:T(4,128)} %param.10) | copy-start | bytes 8068
  11.1 51.8 %all-to-all-start = ((bf16[512,4,512]{0,2,1:T(8,128)(2,1)}), bf16[512,4,512]{0,2,1:T(8,128)(2,1)S(1)}, u32[]{:S(2)}, u32[]{:S(2)}) async-start(bf16[512,4,512]{0,2,1:T(8,128)(2,1)} %bitcast.300), calls=%async_computation | async-start | bytes 4194304 | tf_op jit(solution)/shard_map/all_to_all | solution.py:46
  20.1 81.7 %collective-permute-start = (bf16[512,512]{0,1:T(8,128)(2,1)}, bf16[512,512]{0,1:T(8,128)(2,1)}, u32[]{:S(2)}, u32[]{:S(2)}) collective-permute-start(bf16[512,512]{0,1:T(8,128)(2,1)} %copy.325), channel_id=1, source_target_pairs={{0,1},{1,0},{2,3},{3,2},{4,5},{5,4},{6,7},{7,6},{8,9},{9,8},{10,11... | collective-permute-start | bytes 1572872 | tf_op jit(solution)/shard_map/ppermute | solution.py:21
  22.6 80.3 %collective-permute-start.1 = (bf16[512,512]{0,1:T(8,128)(2,1)}, bf16[512,512]{0,1:T(8,128)(2,1)}, u32[]{:S(2)}, u32[]{:S(2)}) collective-permute-start(bf16[512,512]{0,1:T(8,128)(2,1)} %copy.326), channel_id=1, source_target_pairs={{0,2},{1,3},{2,0},{3,1},{4,6},{5,7},{6,4},{7,5},{8,10},{9,11},{10,... | collective-permute-start | bytes 1572872 | tf_op jit(solution)/shard_map/ppermute | solution.py:21
  25.5 78.5 %collective-permute-start.2 = (bf16[512,512]{0,1:T(8,128)(2,1)}, bf16[512,512]{0,1:T(8,128)(2,1)}, u32[]{:S(2)}, u32[]{:S(2)}) collective-permute-start(bf16[512,512]{0,1:T(8,128)(2,1)} %copy.327), channel_id=1, source_target_pairs={{0,3},{1,2},{2,1},{3,0},{4,7},{5,6},{6,5},{7,4},{8,11},{9,10},{10,... | collective-permute-start | bytes 1572872 | tf_op jit(solution)/shard_map/ppermute | solution.py:21
  40.7 10.5 %copy-start.128 = (s32[32]{0:T(128)S(1)}, s32[32]{0:T(128)}, u32[]{:S(2)}) copy-start(s32[32]{0:T(128)} %param.11) | copy-start | bytes 388
  64.2 29.7 %all-to-all-start.1 = ((bf16[512,4,512]{0,2,1:T(8,128)(2,1)}), bf16[512,4,512]{0,2,1:T(8,128)(2,1)S(1)}, u32[]{:S(2)}, u32[]{:S(2)}) async-start(bf16[512,4,512]{0,2,1:T(8,128)(2,1)} %bitcast.302), calls=%async_computation.1 | async-start | bytes 4194304 | tf_op jit(solution)/shard_map/all_to_all | solution.py:47
  93.9 30.2 %all-to-all-start.2 = ((bf16[512,4,512]{0,2,1:T(8,128)(2,1)}), bf16[512,4,512]{0,2,1:T(8,128)(2,1)}, u32[]{:S(2)}, u32[]{:S(2)}) async-start(bf16[512,4,512]{0,2,1:T(8,128)(2,1)} %bitcast.301), calls=%async_computation.2 | async-start | bytes 4194304 | tf_op jit(solution)/shard_map/all_to_all | solution.py:49
  98.4 244.0 %all-gather.2.cloned.1.call-start = ((), (), s32[]{:S(2)}) async-start(), calls=%async_computation.7 | async-start | bytes 3932160 | tf_op jit(solution)/shard_map/all_gather | solution.py:132
  133.2 14.3 %copy-start.38 = (bf16[1,512,512]{1,2,0:T(8,128)(2,1)S(1)}, bf16[1,512,512]{1,2,0:T(8,128)(2,1)}, u32[]{:S(2)}) copy-start(bf16[1,512,512]{1,2,0:T(8,128)(2,1)} %get-tuple-element.19) | copy-start | bytes 1572868
  133.2 14.3 %copy-start.71 = (pred[512,1024]{1,0:T(8,128)(4,1)S(1)}, pred[512,1024]{1,0:T(8,128)(4,1)}, u32[]{:S(2)}) copy-start(pred[512,1024]{1,0:T(8,128)(4,1)} %get-tuple-element.85) | copy-start | bytes 1572868
  133.2 14.3 %copy-start.72 = (pred[512,1024]{1,0:T(8,128)(4,1)S(1)}, pred[512,1024]{1,0:T(8,128)(4,1)}, u32[]{:S(2)}) copy-start(pred[512,1024]{1,0:T(8,128)(4,1)} %get-tuple-element.86) | copy-start | bytes 1572868
  133.2 14.3 %copy-start.73 = (pred[512,1024]{1,0:T(8,128)(4,1)S(1)}, pred[512,1024]{1,0:T(8,128)(4,1)}, u32[]{:S(2)}) copy-start(pred[512,1024]{1,0:T(8,128)(4,1)} %get-tuple-element.87) | copy-start | bytes 1572868
  133.2 14.3 %copy-start.74 = (pred[512,1024]{1,0:T(8,128)(4,1)S(1)}, pred[512,1024]{1,0:T(8,128)(4,1)}, u32[]{:S(2)}) copy-start(pred[512,1024]{1,0:T(8,128)(4,1)} %get-tuple-element.88) | copy-start | bytes 1572868
  133.2 14.3 %copy-start.75 = (pred[512,1024]{1,0:T(8,128)(4,1)S(1)}, pred[512,1024]{1,0:T(8,128)(4,1)}, u32[]{:S(2)}) copy-start(pred[512,1024]{1,0:T(8,128)(4,1)} %get-tuple-element.89) | copy-start | bytes 1572868
  133.2 14.3 %copy-start.76 = (pred[512,1024]{1,0:T(8,128)(4,1)S(1)}, pred[512,1024]{1,0:T(8,128)(4,1)}, u32[]{:S(2)}) copy-start(pred[512,1024]{1,0:T(8,128)(4,1)} %get-tuple-element.90) | copy-start | bytes 1572868
  133.2 14.3 %copy-start.77 = (pred[512,1024]{1,0:T(8,128)(4,1)S(1)}, pred[512,1024]{1,0:T(8,128)(4,1)}, u32[]{:S(2)}) copy-start(pred[512,1024]{1,0:T(8,128)(4,1)} %get-tuple-element.91) | copy-start | bytes 1572868
  133.2 14.3 %copy-start.78 = (pred[512,1024]{1,0:T(8,128)(4,1)S(1)}, pred[512,1024]{1,0:T(8,128)(4,1)}, u32[]{:S(2)}) copy-start(pred[512,1024]{1,0:T(8,128)(4,1)} %get-tuple-element.92) | copy-start | bytes 1572868
  133.2 14.3 %copy-start.79 = (pred[512,1024]{1,0:T(8,128)(4,1)S(1)}, pred[512,1024]{1,0:T(8,128)(4,1)}, u32[]{:S(2)}) copy-start(pred[512,1024]{1,0:T(8,128)(4,1)} %get-tuple-element.93) | copy-start | bytes 1572868
  133.3 14.3 %copy-start.80 = (pred[512,1024]{1,0:T(8,128)(4,1)S(1)}, pred[512,1024]{1,0:T(8,128)(4,1)}, u32[]{:S(2)}) copy-start(pred[512,1024]{1,0:T(8,128)(4,1)} %get-tuple-element.94) | copy-start | bytes 1572868
  133.3 14.3 %copy-start.81 = (pred[512,1024]{1,0:T(8,128)(4,1)S(1)}, pred[512,1024]{1,0:T(8,128)(4,1)}, u32[]{:S(2)}) copy-start(pred[512,1024]{1,0:T(8,128)(4,1)} %get-tuple-element.95) | copy-start | bytes 1572868
  133.3 14.3 %copy-start.82 = (pred[512,1024]{1,0:T(8,128)(4,1)S(1)}, pred[512,1024]{1,0:T(8,128)(4,1)}, u32[]{:S(2)}) copy-start(pred[512,1024]{1,0:T(8,128)(4,1)} %get-tuple-element.96) | copy-start | bytes 1572868
  133.3 14.3 %copy-start.83 = (pred[512,1024]{1,0:T(8,128)(4,1)S(1)}, pred[512,1024]{1,0:T(8,128)(4,1)}, u32[]{:S(2)}) copy-start(pred[512,1024]{1,0:T(8,128)(4,1)} %get-tuple-element.97) | copy-start | bytes 1572868
  169.2 20.6 %copy-start.31 = (bf16[1,512,512]{1,2,0:T(8,128)(2,1)S(1)}, bf16[1,512,512]{1,2,0:T(8,128)(2,1)}, u32[]{:S(2)}) copy-start(bf16[1,512,512]{1,2,0:T(8,128)(2,1)} %get-tuple-element.18) | copy-start | bytes 1572868
  169.2 20.6 %copy-start.41 = (bf16[1536,4,128]{0,2,1:T(8,128)(2,1)S(1)}, bf16[1536,4,128]{0,2,1:T(8,128)(2,1)}, u32[]{:S(2)}) copy-start(bf16[1536,4,128]{0,2,1:T(8,128)(2,1)} %reshape.1378) | copy-start | bytes 4718596
  169.2 20.6 %copy-start.58 = (pred[512,1536]{1,0:T(8,128)(4,1)S(1)}, pred[512,1536]{1,0:T(8,128)(4,1)}, u32[]{:S(2)}) copy-start(pred[512,1536]{1,0:T(8,128)(4,1)} %get-tuple-element.72) | copy-start | bytes 2359300
  169.2 20.6 %copy-start.59 = (pred[512,1536]{1,0:T(8,128)(4,1)S(1)}, pred[512,1536]{1,0:T(8,128)(4,1)}, u32[]{:S(2)}) copy-start(pred[512,1536]{1,0:T(8,128)(4,1)} %get-tuple-element.73) | copy-start | bytes 2359300
  169.2 20.6 %copy-start.60 = (pred[512,1536]{1,0:T(8,128)(4,1)S(1)}, pred[512,1536]{1,0:T(8,128)(4,1)}, u32[]{:S(2)}) copy-start(pred[512,1536]{1,0:T(8,128)(4,1)} %get-tuple-element.74) | copy-start | bytes 2359300
  169.2 20.6 %copy-start.61 = (pred[512,1536]{1,0:T(8,128)(4,1)S(1)}, pred[512,1536]{1,0:T(8,128)(4,1)}, u32[]{:S(2)}) copy-start(pred[512,1536]{1,0:T(8,128)(4,1)} %get-tuple-element.75) | copy-start | bytes 2359300
  169.2 20.6 %copy-start.62 = (pred[512,1536]{1,0:T(8,128)(4,1)S(1)}, pred[512,1536]{1,0:T(8,128)(4,1)}, u32[]{:S(2)}) copy-start(pred[512,1536]{1,0:T(8,128)(4,1)} %get-tuple-element.76) | copy-start | bytes 2359300
  169.2 20.6 %copy-start.63 = (pred[512,1536]{1,0:T(8,128)(4,1)S(1)}, pred[512,1536]{1,0:T(8,128)(4,1)}, u32[]{:S(2)}) copy-start(pred[512,1536]{1,0:T(8,128)(4,1)} %get-tuple-element.77) | copy-start | bytes 2359300
  169.2 20.6 %copy-start.64 = (pred[512,1536]{1,0:T(8,128)(4,1)S(1)}, pred[512,1536]{1,0:T(8,128)(4,1)}, u32[]{:S(2)}) copy-start(pred[512,1536]{1,0:T(8,128)(4,1)} %get-tuple-element.78) | copy-start | bytes 2359300
  169.2 20.6 %copy-start.65 = (pred[512,1536]{1,0:T(8,128)(4,1)S(1)}, pred[512,1536]{1,0:T(8,128)(4,1)}, u32[]{:S(2)}) copy-start(pred[512,1536]{1,0:T(8,128)(4,1)} %get-tuple-element.79) | copy-start | bytes 2359300
  169.2 20.6 %copy-start.66 = (pred[512,1536]{1,0:T(8,128)(4,1)S(1)}, pred[512,1536]{1,0:T(8,128)(4,1)}, u32[]{:S(2)}) copy-start(pred[512,1536]{1,0:T(8,128)(4,1)} %get-tuple-element.80) | copy-start | bytes 2359300
  169.2 20.6 %copy-start.67 = (pred[512,1536]{1,0:T(8,128)(4,1)S(1)}, pred[512,1536]{1,0:T(8,128)(4,1)}, u32[]{:S(2)}) copy-start(pred[512,1536]{1,0:T(8,128)(4,1)} %get-tuple-element.81) | copy-start | bytes 2359300
  169.2 20.6 %copy-start.68 = (pred[512,1536]{1,0:T(8,128)(4,1)S(1)}, pred[512,1536]{1,0:T(8,128)(4,1)}, u32[]{:S(2)}) copy-start(pred[512,1536]{1,0:T(8,128)(4,1)} %get-tuple-element.82) | copy-start | bytes 2359300
  169.3 20.6 %copy-start.69 = (pred[512,1536]{1,0:T(8,128)(4,1)S(1)}, pred[512,1536]{1,0:T(8,128)(4,1)}, u32[]{:S(2)}) copy-start(pred[512,1536]{1,0:T(8,128)(4,1)} %get-tuple-element.83) | copy-start | bytes 2359300
  169.3 20.6 %copy-start.70 = (pred[512,1536]{1,0:T(8,128)(4,1)S(1)}, pred[512,1536]{1,0:T(8,128)(4,1)}, u32[]{:S(2)}) copy-start(pred[512,1536]{1,0:T(8,128)(4,1)} %get-tuple-element.84) | copy-start | bytes 2359300
  189.9 17.0 %copy-start.20 = (bf16[1536,512]{0,1:T(8,128)(2,1)S(1)}, bf16[1536,512]{0,1:T(8,128)(2,1)}, u32[]{:S(2)}) copy-start(bf16[1536,512]{0,1:T(8,128)(2,1)} %slice.572) | copy-start | bytes 4718596
  237.6 10.0 %copy-start.13 = (bf16[4,512,1024]{2,1,0:T(8,128)(2,1)S(1)}, bf16[4,512,1024]{2,1,0:T(8,128)(2,1)}, u32[]{:S(2)}) copy-start(bf16[4,512,1024]{2,1,0:T(8,128)(2,1)} %fusion.2) | copy-start | bytes 12582916
  317.6 26.1 %copy-start.125 = (s32[2]{0:T(128)S(1)}, s32[2]{0:T(128)}, u32[]{:S(2)}) copy-start(s32[2]{0:T(128)} %copy-done.124) | copy-start | bytes 28
  317.6 26.1 %copy-start.126 = (pred[2]{0:T(512)(128)(4,1)S(1)}, pred[2]{0:T(512)(128)(4,1)}, u32[]{:S(2)}) copy-start(pred[2]{0:T(512)(128)(4,1)} %get-tuple-element.127) | copy-start | bytes 10
  317.6 26.1 %copy-start.127 = (s32[2]{0:T(128)S(1)}, s32[2]{0:T(128)}, u32[]{:S(2)}) copy-start(s32[2]{0:T(128)} %get-tuple-element.124) | copy-start | bytes 28
  343.8 11.1 %copy-start.12 = (bf16[32,64,4,128]{3,2,1,0:T(4,128)(2,1)S(1)}, bf16[32,64,4,128]{3,2,1,0:T(4,128)(2,1)}, u32[]{:S(2)}) copy-start(bf16[32,64,4,128]{3,2,1,0:T(4,128)(2,1)} %reshape_reshape.6) | copy-start | bytes 6291460
  375.7 40.4 %all-to-all-start.3 = ((bf16[4,512,512]{2,1,0:T(8,128)(2,1)}), bf16[4,512,512]{2,1,0:T(8,128)(2,1)}, u32[]{:S(2)}, u32[]{:S(2)}) async-start(bf16[4,512,512]{2,1,0:T(8,128)(2,1)} %add_convert_fusion.1), calls=%async_computation.3 | async-start | bytes 4194304 | tf_op jit(solution)/shard_map/all_to_all | solution.py:172
  416.1 40.9 %all-to-all-start.6 = ((bf16[4,512,512]{2,1,0:T(8,128)(2,1)}), bf16[4,512,512]{2,1,0:T(8,128)(2,1)}, u32[]{:S(2)}, u32[]{:S(2)}) async-start(bf16[4,512,512]{2,1,0:T(8,128)(2,1)} %all_to_all.107), calls=%async_computation.6 | async-start | bytes 4194304 | tf_op jit(solution)/shard_map/all_to_all | solution.py:175
  457.0 32.8 %all-to-all-start.4 = ((bf16[4,512,512]{2,1,0:T(8,128)(2,1)}), bf16[4,512,512]{2,1,0:T(8,128)(2,1)}, u32[]{:S(2)}, u32[]{:S(2)}) async-start(bf16[4,512,512]{2,1,0:T(8,128)(2,1)} %add_convert_fusion), calls=%async_computation.4 | async-start | bytes 4194304 | tf_op jit(solution)/shard_map/all_to_all | solution.py:173
  489.8 29.3 %all-to-all-start.5 = ((bf16[4,512,512]{2,1,0:T(8,128)(2,1)}), bf16[4,512,512]{2,1,0:T(8,128)(2,1)S(1)}, u32[]{:S(2)}, u32[]{:S(2)}) async-start(bf16[4,512,512]{2,1,0:T(8,128)(2,1)} %all_to_all.103), calls=%async_computation.5 | async-start | bytes 4194304 | tf_op jit(solution)/shard_map/all_to_all | solution.py:174
  (92 other events, 606.7 us)
Sparse Core Ops, SparseCore 0:
  262.4 64.3 all-gather.1
